TPU v7x, 512 devices: a whole 4x4x16 slice. The times are simulated.
512 devices in a mesh: seq: 32 (over z, core), tp: 4 (over y), dp: 4 (over x).
Axes of the slice: x: 4, y: 4, z: 16, core: 2. Of those that a mesh axis runs over, the one named last changes fastest.
Arguments:
- queries: bfloat16 [4, 8192, 2048], P(None, 'seq', ('tp', 'dp')), may hold values from -64 to 64
- block_states: bfloat16 [4, 8192, 2048], P(None, 'seq', ('tp', 'dp')), may hold values from -40 to 40
- grad_out: bfloat16 [4, 8192, 2048], P(None, 'seq', ('tp', 'dp')), may hold values from -6 to 6
- store: bfloat16 [1024, 128, 2048], P('seq', None, ('tp', 'dp')), may hold values from -40 to 40
- owners: int32 [128, 4, 2], P('seq'), may hold values from 0 to 31, all different within a row; in each aligned block of 16 rows (0 to 15, 16 to 31, ..., all dimensions but the last counted through in order) at most 2 rows name the same one
- entries: int32 [128, 4, 2], P('seq'), may hold values from 0 to 31
Outputs:
- attended: bfloat16 [4, 8192, 2048], P(None, 'seq', ('tp', 'dp'))
- query_grad: bfloat16 [4, 8192, 2048], P(None, 'seq', ('tp', 'dp'))
- state_grad: bfloat16 [4, 8192, 2048], P(None, 'seq', ('tp', 'dp'))
Inputs may be any that keep to these rules, and one draw needn't show every extreme that they name: Within the rows of one device (aligned blocks of 16 rows), no owner is named more than 2 times, a bound that some block reaches; the 2 neighbours of a block name different owners.
All inputs are finite; a program needn't handle non-finite values.
Results may differ from a plain program's by a relative error of at most 0.01295.
Values may be sent and summed in bfloat16 or wider, within the bound.
A program may use at most 64 MiB of HBM per device.

v0:
```python
import jax
import jax.numpy as jnp
from jax import lax
from jax.sharding import PartitionSpec as P

DE = 2048
HD = 128
BLOCK = 64
NLEN = 128
NBR = 2


norm_eps = 1e-06


def passed_along(block, axis, distance):
    devices = range(lax.axis_size(axis))
    route = [(i - distance, i) for i in devices if i - distance in devices]
    return lax.ppermute(block, axis, route)


def softmax_rows(scores):
    row_top = jnp.max(scores, axis=-1, keepdims=True)
    raised = jnp.exp(scores - row_top)
    return raised / jnp.sum(raised, axis=-1, keepdims=True)


def split_heads(values):
    return values.reshape(values.shape[:-1] + (values.shape[-1] // HD, HD))


def encode_rows(neighbours, states, score_scale):
    scores = (
        jnp.einsum("...qhd,...khd->...hqk", neighbours, states, preferred_element_type=jnp.float32)
        * score_scale
    )
    weights = softmax_rows(scores)
    low_weights = weights.astype(jnp.bfloat16)
    mixture = jnp.einsum(
        "...hqk,...khd->...qhd", low_weights, states, preferred_element_type=jnp.float32
    )
    summed = neighbours.astype(jnp.float32) + mixture
    squares = lax.psum(jnp.sum(summed * summed, axis=(-2, -1)), ("tp", "dp"))
    inverse = lax.rsqrt(squares / DE + norm_eps)[..., None, None]
    normed = summed * inverse
    return (normed.astype(jnp.bfloat16), (weights, low_weights, normed, inverse))


def encode_grads(neighbours, states, grad_rows, kept_state, score_scale):
    weights, low_weights, normed, inverse = kept_state
    grad_full = grad_rows.astype(jnp.float32)
    projection = lax.psum(
        jnp.sum(grad_full * normed, axis=(-2, -1)).astype(jnp.bfloat16), ("tp", "dp")
    ).astype(jnp.float32)
    summed_grad = (inverse * (grad_full - normed * (projection / DE)[..., None, None])).astype(
        jnp.bfloat16
    )
    weight_grad = jnp.einsum(
        "...qhd,...khd->...hqk", summed_grad, states, preferred_element_type=jnp.float32
    )
    score_grad = (
        weights * (weight_grad - jnp.sum(weight_grad * weights, axis=-1, keepdims=True))
    ).astype(jnp.bfloat16)
    state_term = jnp.einsum(
        "...hqk,...qhd->...khd", low_weights, summed_grad, preferred_element_type=jnp.float32
    )
    state_term = state_term + score_scale * jnp.einsum(
        "...hqk,...qhd->...khd", score_grad, neighbours, preferred_element_type=jnp.float32
    )
    return state_term.astype(jnp.bfloat16)


def on_device(queries, block_states, grad_out, store, owners, entries):
    members = lax.axis_size("seq")
    batch_seqs, tok_rows, columns = queries.shape
    blk_count = tok_rows // BLOCK
    score_scale = HD ** (-0.5)
    blk_rows = blk_count * batch_seqs
    capacity = min(blk_rows, max(2, (4 * blk_rows + members - 1) // members))
    item_count = blk_rows * NBR
    flat_owner = owners.reshape(item_count)
    flat_entry = entries.reshape(item_count)
    owner_lanes = jnp.arange(members, dtype=jnp.int32)
    owner_hot = (flat_owner[:, None] == owner_lanes[None, :]).astype(jnp.int32)
    before = jnp.cumsum(owner_hot, axis=0) - owner_hot
    slot_rank = jnp.sum(before * owner_hot, axis=1)
    target = flat_owner * capacity + slot_rank
    slot_cells = jnp.arange(members * capacity, dtype=jnp.int32)
    placement = slot_cells[:, None] == target[None, :]
    place_low = placement.astype(jnp.bfloat16)
    pick_rows = jnp.sum(
        placement.reshape(members * capacity, blk_count, batch_seqs, NBR).astype(jnp.float32),
        axis=-1,
    ).astype(jnp.bfloat16)
    send_ids = jnp.sum(jnp.where(placement, flat_entry[None, :], 0), axis=1).reshape(
        members, capacity
    )
    states_four = block_states.reshape(batch_seqs, blk_count, BLOCK, columns)
    send_states = (
        jnp.einsum("zjb,bjcw->zcw", pick_rows, states_four, preferred_element_type=jnp.float32)
        .astype(jnp.bfloat16)
        .reshape(members, capacity, BLOCK, columns)
    )
    states_in = lax.all_to_all(send_states, "seq", split_axis=0, concat_axis=0, tiled=True)
    ids_in = lax.all_to_all(send_ids, "seq", split_axis=0, concat_axis=0, tiled=True)
    neighbours = split_heads(store[ids_in])
    encoded, kept_state = encode_rows(neighbours, split_heads(states_in), score_scale)
    returned_rows = lax.all_to_all(
        encoded.reshape(ids_in.shape + (NLEN, columns)),
        "seq",
        split_axis=0,
        concat_axis=0,
        tiled=True,
    )
    key_items = jnp.einsum(
        "zi,zlw->ilw",
        place_low,
        returned_rows.reshape(members * capacity, NLEN, columns),
        preferred_element_type=jnp.float32,
    ).astype(jnp.bfloat16)
    key_rows = key_items.reshape(blk_count, batch_seqs, NBR * NLEN, columns)
    previous = passed_along(key_rows[blk_count - 1], "seq", 1)
    extended = split_heads(jnp.concatenate([previous[None], key_rows], axis=0))
    padding = ((0, 0), (1, BLOCK - 1), (0, 0))
    query_blocks = split_heads(
        jnp.pad(queries, padding).reshape(batch_seqs, blk_count + 1, BLOCK, columns)
    )
    grad_blocks = split_heads(
        jnp.pad(grad_out, padding).reshape(batch_seqs, blk_count + 1, BLOCK, columns)
    )
    scores = (
        jnp.einsum("bgqhd,gbkhd->bghqk", query_blocks, extended, preferred_element_type=jnp.float32)
        * score_scale
    )
    weights = softmax_rows(scores)
    low_weights = weights.astype(jnp.bfloat16)
    attended = jnp.einsum(
        "bghqk,gbkhd->bgqhd", low_weights, extended, preferred_element_type=jnp.float32
    ).astype(jnp.bfloat16)
    weight_grad = jnp.einsum(
        "bgqhd,gbkhd->bghqk", grad_blocks, extended, preferred_element_type=jnp.float32
    )
    score_grad = (
        weights * (weight_grad - jnp.sum(weight_grad * weights, axis=-1, keepdims=True))
    ).astype(jnp.bfloat16)
    query_grad = (
        score_scale
        * jnp.einsum("bghqk,gbkhd->bgqhd", score_grad, extended, preferred_element_type=jnp.float32)
    ).astype(jnp.bfloat16)
    key_grad = jnp.einsum(
        "bghqk,bgqhd->gbkhd", low_weights, grad_blocks, preferred_element_type=jnp.float32
    )
    key_grad = key_grad + score_scale * jnp.einsum(
        "bghqk,bgqhd->gbkhd", score_grad, query_blocks, preferred_element_type=jnp.float32
    )
    returned = passed_along(key_grad[0].astype(jnp.bfloat16), "seq", -1).astype(jnp.float32)
    local_grad = key_grad[1:].at[blk_count - 1].add(returned).astype(jnp.bfloat16)
    send_grads = (
        jnp.einsum(
            "zi,ilw->zlw",
            place_low,
            local_grad.reshape(item_count, NLEN, columns),
            preferred_element_type=jnp.float32,
        )
        .astype(jnp.bfloat16)
        .reshape(members, capacity, NLEN, columns)
    )
    states_in = lax.all_to_all(send_states, "seq", split_axis=0, concat_axis=0, tiled=True)
    ids_in = lax.all_to_all(send_ids, "seq", split_axis=0, concat_axis=0, tiled=True)
    grads_in = lax.all_to_all(send_grads, "seq", split_axis=0, concat_axis=0, tiled=True)
    neighbours = split_heads(store[ids_in])
    state_split = split_heads(states_in)
    encoded_again, kept_again = encode_rows(neighbours, state_split, score_scale)
    state_term = encode_grads(
        neighbours, state_split, split_heads(grads_in), kept_again, score_scale
    )
    terms_home = lax.all_to_all(
        state_term.reshape(ids_in.shape + (BLOCK, columns)),
        "seq",
        split_axis=0,
        concat_axis=0,
        tiled=True,
    )
    state_sum = jnp.einsum(
        "zjb,zcw->bjcw",
        pick_rows,
        terms_home.reshape(members * capacity, BLOCK, columns),
        preferred_element_type=jnp.float32,
    )
    state_grad = state_sum.astype(jnp.bfloat16).reshape(batch_seqs, tok_rows, columns)
    attended_rows = attended.reshape(batch_seqs, (blk_count + 1) * BLOCK, columns)[
        :, 1 : 1 + tok_rows
    ]
    query_rows = query_grad.reshape(batch_seqs, (blk_count + 1) * BLOCK, columns)[
        :, 1 : 1 + tok_rows
    ]
    return (attended_rows, query_rows, state_grad)


def solution(mesh):
    placed = (
        P(None, "seq", ("tp", "dp")),
        P(None, "seq", ("tp", "dp")),
        P(None, "seq", ("tp", "dp")),
        P("seq", None, ("tp", "dp")),
        P("seq", None, None),
        P("seq", None, None),
    )
    return jax.shard_map(
        on_device,
        mesh=mesh,
        in_specs=placed,
        out_specs=(
            P(None, "seq", ("tp", "dp")),
            P(None, "seq", ("tp", "dp")),
            P(None, "seq", ("tp", "dp")),
        ),
        check_vma=False,
    )
```

profile of v0, /device:TPU:1, one launch (start us, length us, event | category | flops | bytes accessed | tf_op | source)
XLA Modules:
  0.0 587.5 jit_solution(17313484470094053231)
XLA Ops:
  3.7 16.7 %all-to-all-start = ((s32[32,1,2]{2,1,0:T(1,128)}), s32[32,1,2]{2,1,0:T(1,128)S(1)}, u32[]{:S(2)}, u32[]{:S(2)}) async-start(s32[32,1,2]{2,1,0:T(1,128)} %bitcast.1), calls=%async_computation | async-start | bytes 32768 | tf_op jit(solution)/shard_map/all_to_all | solution.py:105
  22.9 2.2 copy.126
  25.1 7.0 %all-to-all-done = s32[32,1,2]{2,1,0:T(1,128)S(1)} async-done(((s32[32,1,2]{2,1,0:T(1,128)}), s32[32,1,2]{2,1,0:T(1,128)S(1)}, u32[]{:S(2)}, u32[]{:S(2)}) %all-to-all-start) | async-done | bytes 288 | tf_op jit(solution)/shard_map/all_to_all | solution.py:105
  32.1 5.2 all-to-all-start.1
  38.7 3.0 copy.121
  41.6 51.5 %all-to-all-done.1 = bf16[32,2,64,128]{3,2,1,0:T(8,128)(2,1)} async-done(((bf16[32,2,64,128]{3,2,1,0:T(8,128)(2,1)}), bf16[32,2,64,128]{3,2,1,0:T(8,128)(2,1)}, u32[]{:S(2)}, u32[]{:S(2)}) %all-to-all-start.1) | async-done | bytes 1048608 | tf_op jit(solution)/shard_map/all_to_all | solution.py:104
  93.2 2.7 fusion.59
  95.9 2.0 fusion.55
  97.9 6.0 %multiply_reduce_fusion = (f32[32,2,128]{2,1,0:T(2,128)S(1)}, f32[32,2,128,1,128]{2,4,1,0,3:T(8,128)}) fusion(bf16[32,2,64,128]{3,2,1,0:T(8,128)(2,1)} %all-to-all-done.1, f32[32,2,128]{2,1,0:T(2,128)S(1)} %get-tuple-element.17, f32[32,2,128,64]{2,3,1,0:T(8,128)} %copy-done.3, bf16[32,2,128,1,128]{2,4,1,0,3:T(8,128)(2,1)} %bitcast.101), kind=kOutput, calls=%fused_computation.9 | convolution fusion | flops 140509248 | bytes 9502720 | tf_op jit(solution)/shard_map/...hqk,...khd->...qhd/dot_general | solution.py:39
  103.9 60.4 %psum.14 = f32[32,2,128]{2,1,0:T(2,128)S(1)} all-reduce(f32[32,2,128]{2,1,0:T(2,128)S(1)} %get-tuple-element.19), channel_id=1, replica_groups=mesh['seq'=32,'tp'=4,'dp'=4] {'tp','dp'}, use_global_device_ids=true, to_apply=%region_7.8 | all-reduce | flops 8192 | bytes 65536 | tf_op jit(solution)/shard_map/psum | solution.py:43
  164.3 2.8 fusion.5
  167.1 118.8 %all_to_all.34 = bf16[32,2,128,128]{2,3,1,0:T(8,128)(2,1)} all-to-all(bf16[32,2,128,128]{2,3,1,0:T(8,128)(2,1)S(1)} %fusion.5), channel_id=1, replica_groups=mesh['seq'=32,'tp'=4,'dp'=4] {'seq'}, dimensions={0} | all-to-all | bytes 4194304 | tf_op jit(solution)/shard_map/all_to_all | solution.py:108
  285.9 4.1 copy.128
  290.1 2.1 convolution_convert_fusion.1
  292.3 2.1 collective-permute-start
  298.2 3.2 fusion.58
  301.4 2.6 multiply_reduce_fusion.3
  306.1 1.9 collective-permute-start.1
  309.2 5.4 collective-permute-done.1
  315.4 2.3 copy.138
  317.6 3.6 convolution_convert_fusion
  321.3 4.2 copy.140
  325.4 106.6 %all_to_all.35 = bf16[32,2,128,128]{2,3,1,0:T(8,128)(2,1)S(1)} all-to-all(bf16[32,2,128,128]{2,3,1,0:T(8,128)(2,1)} %bitcast.96), channel_id=1, replica_groups=mesh['seq'=32,'tp'=4,'dp'=4] {'seq'}, dimensions={0} | all-to-all | bytes 4194304 | tf_op jit(solution)/shard_map/all_to_all | solution.py:170
  434.3 56.1 %psum.18 = bf16[32,2,128]{2,1,0:T(2,128)(2,1)S(1)} all-reduce(bf16[32,2,128]{2,1,0:T(2,128)(2,1)S(1)} %fusion.2), channel_id=1, replica_groups=mesh['seq'=32,'tp'=4,'dp'=4] {'tp','dp'}, use_global_device_ids=true, to_apply=%region_12.13 | all-reduce | flops 8192 | bytes 32768 | tf_op jit(solution)/shard_map/psum | solution.py:52
  490.5 5.3 fusion.6
  495.8 5.1 fusion.22
  500.9 4.5 multiply_reduce_fusion.1
  505.4 5.1 fusion.10
  510.5 18.3 %all-to-all-start.4 = ((bf16[32,2,64,128]{3,2,1,0:T(8,128)(2,1)}), bf16[32,2,64,128]{3,2,1,0:T(8,128)(2,1)}, u32[]{:S(2)}, u32[]{:S(2)}) async-start(bf16[32,2,64,128]{3,2,1,0:T(8,128)(2,1)} %fusion.10), calls=%async_computation.4 | async-start | bytes 2097152 | tf_op jit(solution)/shard_map/all_to_all | solution.py:177
  528.9 1.7 convolution_convert_fusion.2
  532.5 52.2 %all-to-all-done.4 = bf16[32,2,64,128]{3,2,1,0:T(8,128)(2,1)} async-done(((bf16[32,2,64,128]{3,2,1,0:T(8,128)(2,1)}), bf16[32,2,64,128]{3,2,1,0:T(8,128)(2,1)}, u32[]{:S(2)}, u32[]{:S(2)}) %all-to-all-start.4) | async-done | bytes 1048608 | tf_op jit(solution)/shard_map/all_to_all | solution.py:177
  584.7 2.0 fusion.12
  (79 shorter events, 19.6 us)
Async XLA Ops:
  0.6 37.1 %copy-start = (bf16[32,128,128]{2,1,0:T(8,128)(2,1)S(1)}, bf16[32,128,128]{2,1,0:T(8,128)(2,1)}, u32[]{:S(2)}) copy-start(bf16[32,128,128]{2,1,0:T(8,128)(2,1)} %param.11) | copy-start | bytes 3145732
  2.8 287.2 %copy-start.15 = (s32[32]{0:T(128)}, s32[32]{0:T(128)S(1)}, u32[]{:S(2)}) copy-start(s32[32]{0:T(128)S(1)} %multiply_add_fusion.1) | copy-start | bytes 388
  3.7 28.5 %all-to-all-start = ((s32[32,1,2]{2,1,0:T(1,128)}), s32[32,1,2]{2,1,0:T(1,128)S(1)}, u32[]{:S(2)}, u32[]{:S(2)}) async-start(s32[32,1,2]{2,1,0:T(1,128)} %bitcast.1), calls=%async_computation | async-start | bytes 32768 | tf_op jit(solution)/shard_map/all_to_all | solution.py:105
  21.4 3.7 copy-start.13
  32.1 61.0 %all-to-all-start.1 = ((bf16[32,2,64,128]{3,2,1,0:T(8,128)(2,1)}), bf16[32,2,64,128]{3,2,1,0:T(8,128)(2,1)}, u32[]{:S(2)}, u32[]{:S(2)}) async-start(bf16[32,2,64,128]{3,2,1,0:T(8,128)(2,1)} %copy.126), calls=%async_computation.1 | async-start | bytes 2097152 | tf_op jit(solution)/shard_map/all_to_all | solution.py:104
  95.9 2.0 copy-start.3
  290.1 4.3 copy-start.11
  290.1 4.4 copy-start.12
  292.3 5.2 collective-permute-start
  297.5 0.7 copy-start.17
  301.4 2.6 copy-start.8
  304.0 1.0 copy-start.9
  304.4 1.1 copy-start.6
  304.4 1.6 copy-start.4
  306.1 8.4 %collective-permute-start.1 = (bf16[4,256,1,128]{1,3,0,2:T(8,128)(2,1)S(1)}, bf16[4,256,1,128]{1,3,0,2:T(8,128)(2,1)S(1)}, u32[]{:S(2)}, u32[]{:S(2)}) collective-permute-start(bf16[4,256,1,128]{1,3,0,2:T(8,128)(2,1)S(1)} %fusion.27), channel_id=1, source_target_pairs={{16,0},{32,16},{48,32},{64,48},{80,64},{96,80},{112,96},{128,112},... | collective-permute-start | bytes 786440 | tf_op jit(solution)/shard_map/ppermute | solution.py:19
  309.2 8.5 %copy-start.16 = (s32[32]{0:T(128)S(1)}, s32[32]{0:T(128)}, u32[]{:S(2)}) copy-start(s32[32]{0:T(128)} %copy-done.15) | copy-start | bytes 388
  325.4 107.9 %copy-start.1 = (f32[32,2,128,1,128]{2,4,1,0,3:T(8,128)S(1)}, f32[32,2,128,1,128]{2,4,1,0,3:T(8,128)}, u32[]{:S(2)}) copy-start(f32[32,2,128,1,128]{2,4,1,0,3:T(8,128)} %get-tuple-element.20) | copy-start | bytes 12582916
  432.1 1.3 copy-start.2
  510.5 18.3 %copy-start.7 = (bf16[4,5,64,256]{3,2,1,0:T(8,128)(2,1)S(1)}, bf16[4,5,64,256]{3,2,1,0:T(8,128)(2,1)}, u32[]{:S(2)}) copy-start(bf16[4,5,64,256]{3,2,1,0:T(8,128)(2,1)} %copy-done.6) | copy-start | bytes 1966084
  510.5 18.3 %copy-start.18 = (bf16[4,256,128]{2,1,0:T(8,128)(2,1)S(1)}, bf16[4,256,128]{2,1,0:T(8,128)(2,1)}, u32[]{:S(2)}) copy-start(bf16[4,256,128]{2,1,0:T(8,128)(2,1)} %copy-done.17) | copy-start | bytes 786436
  510.5 74.2 %all-to-all-start.4 = ((bf16[32,2,64,128]{3,2,1,0:T(8,128)(2,1)}), bf16[32,2,64,128]{3,2,1,0:T(8,128)(2,1)}, u32[]{:S(2)}, u32[]{:S(2)}) async-start(bf16[32,2,64,128]{3,2,1,0:T(8,128)(2,1)} %fusion.10), calls=%async_computation.4 | async-start | bytes 2097152 | tf_op jit(solution)/shard_map/all_to_all | solution.py:177
  528.8 2.5 copy-start.5
  528.9 2.5 copy-start.10
  531.4 53.3 %copy-start.14 = (bf16[64,4,4]{0,2,1:T(4,128)(2,1)S(1)}, bf16[64,4,4]{0,2,1:T(4,128)(2,1)}, u32[]{:S(2)}) copy-start(bf16[64,4,4]{0,2,1:T(4,128)(2,1)} %copy-done.13) | copy-start | bytes 6148
where the time goes:
time: 589 us; the launch traced here: 587 us
  blocking collectives  342 us (58%)
  waiting for transfers between devices  117 us (20%)
  starting transfers between devices  44.3 us (8%)
  matrix products  41.6 us (7%)
  local copies, waits for them, and re-layouts  28.1 us (5%)
  other arithmetic  13.6 us (2%)
    all_to_all x1, blocking collectives, on_device(): lax.all_to_all(encoded.reshape(ids_in.shape + (NLEN, columns)), 'seq', sp...  119 us
    all_to_all x1, blocking collectives, on_device(): lax.all_to_all(send_grads, 'seq', split_axis=0, concat_axis=0, tiled=True)  107 us
    psum x1, blocking collectives, encode_rows(): squares = lax.psum(jnp.sum(summed * summed, axis=(-2, -1)), ('tp', 'dp'))  60.4 us
    psum x1, blocking collectives, encode_grads(): lax.psum(jnp.sum(grad_full * normed, axis=(-2, -1)).astype(jnp.bfloat16),...  56.1 us
    all_to_all x1, waiting for transfers between devices, on_device(): lax.all_to_all(state_term.reshape(ids_in.shape + (BLOCK, columns)), 'seq'...  52.2 us
    all_to_all x1, waiting for transfers between devices, on_device(): lax.all_to_all(send_states, 'seq', split_axis=0, concat_axis=0, tiled=True)  51.5 us
    all_to_all x1, starting transfers between devices, on_device(): lax.all_to_all(state_term.reshape(ids_in.shape + (BLOCK, columns)), 'seq'...  18.3 us
    all_to_all x1, starting transfers between devices, on_device(): lax.all_to_all(send_ids, 'seq', split_axis=0, concat_axis=0, tiled=True)  16.7 us
  transfers between devices with their start and end apart: 5, of which 5 were waited for; matrix products, arithmetic and copies ran while one was open for 3% of the time, Pallas kernels for 0%

commit v1 on v0

v1 whole, which is shorter than its diff:
```python
import functools

import jax
import jax.numpy as jnp
from jax import lax
from jax.experimental import pallas as pl
from jax.experimental.pallas import tpu as pltpu
from jax.sharding import PartitionSpec as P

HD = 128
BLOCK = 64
NLEN = 128
NBR = 2
SLOTS = 2
norm_eps = 1e-06
MESH = pl.DeviceIdType.MESH
f32 = jnp.float32
bf16 = jnp.bfloat16


def place_distance(place, members):
    turn = members // 2 + (place // 2) * (1 - 2 * ((place + 1) % 2))
    return turn


def nn(a, b):
    return lax.dot_general(a, b, (((1,), (0,)), ((), ())), preferred_element_type=f32)


def nt(a, b):
    return lax.dot_general(a, b, (((1,), (1,)), ((), ())), preferred_element_type=f32)


def shift_matrix(rows, columns, offset):
    i = lax.broadcasted_iota(jnp.int32, (rows, columns), 0)
    j = lax.broadcasted_iota(jnp.int32, (rows, columns), 1)
    return (j == i + offset).astype(f32).astype(bf16)


def kernel(
    members, ntp, ndp, seqs, groups, chunk,
    item_slot, slot_block, own_ids, ids_ref, q_ref, g_ref, s_ref, store_ref,
    att_ref, qg_ref, sg_ref,
    ids_in, ids_s, send, recv, summed, wts, squares, inv, qn, gn, qb, gb, qt, gt, st, atb, qgb, kgrad, proj,
    ids_send, ids_recv, loc_sem, tok_send, tok_recv, data_send, data_recv, sq_send, sq_recv, pr_send, pr_recv,
    o_send, o_recv,
):
    me = lax.axis_index("seq")
    tp = lax.axis_index("tp")
    dp = lax.axis_index("dp")
    peers = ntp * ndp
    scale = HD ** (-0.5)
    width = HD * peers
    after = lax.rem(me + 1, members)
    before = lax.rem(me + members - 1, members)

    def ring(distance):
        return {"seq": lax.rem(me + distance, members)}

    def plane(q):
        return {"tp": lax.rem(tp + q // ndp, ntp), "dp": lax.rem(dp + q % ndp, ndp)}

    barrier = pltpu.get_barrier_semaphore()

    def greet_ring(d, c):
        pl.semaphore_signal(barrier, inc=1, device_id=ring(d), device_id_type=MESH)
        return c

    def greet_plane(q, c):
        pl.semaphore_signal(barrier, inc=1, device_id=plane(q), device_id_type=MESH)
        return c

    lax.fori_loop(1, members, greet_ring, 0)
    lax.fori_loop(1, peers, greet_plane, 0)
    pl.semaphore_wait(barrier, members - 1 + peers - 1)

    def send_ids(d, c):
        pltpu.make_async_remote_copy(
            src_ref=ids_ref, dst_ref=ids_in.at[d], send_sem=ids_send, recv_sem=ids_recv,
            device_id=ring(d), device_id_type=MESH,
        ).start()
        return c

    lax.fori_loop(1, members, send_ids, 0)
    tok_copies = []
    for k, (src, dst) in enumerate(((q_ref, qn), (g_ref, gn))):
        copy = pltpu.make_async_remote_copy(
            src_ref=src.at[:, pl.ds(0, BLOCK)], dst_ref=dst, send_sem=tok_send.at[k], recv_sem=tok_recv.at[k],
            device_id={"seq": before}, device_id_type=MESH,
        )
        copy.start()
        tok_copies.append(copy)

    eye = shift_matrix(HD, HD, 0)

    for k in range(SLOTS):
        recv[k] = store_ref[own_ids[k]]

    def turn_states(i, c):
        st[i] = nt(eye, s_ref[i]).astype(bf16)
        return c

    lax.fori_loop(0, seqs * groups, turn_states, 0)

    pltpu.make_async_copy(ids_in.at[pl.ds(1, members - 1)], ids_in.at[pl.ds(1, members - 1)], ids_recv).wait()
    to_scalar = pltpu.make_async_copy(ids_in.at[pl.ds(1, members - 1)], ids_s.at[pl.ds(1, members - 1)], loc_sem)
    to_scalar.start()
    to_scalar.wait()

    def send_items(p, c):
        d = place_distance(p, members)
        for k in range(SLOTS):
            send[SLOTS * p + k] = store_ref[ids_s[members - d, 0, SLOTS * p + k]]
        pltpu.make_async_remote_copy(
            src_ref=send.at[pl.ds(SLOTS * p, SLOTS)], dst_ref=recv.at[pl.ds(SLOTS * p, SLOTS)],
            send_sem=data_send, recv_sem=data_recv.at[p], device_id=ring(d), device_id_type=MESH,
        ).start()
        return c

    lax.fori_loop(1, members, send_items, 0)

    for copy in tok_copies:
        copy.wait()
    last = (me < members - 1).astype(f32)
    first = (me > 0).astype(f32)
    for b in range(seqs):
        qn[b] = (qn[b].astype(f32) * last).astype(bf16)
        gn[b] = (gn[b].astype(f32) * last).astype(bf16)
    take = shift_matrix(BLOCK, 2 * BLOCK, BLOCK - 1)
    for b in range(seqs):
        for g in range(groups):
            i = b * groups + g
            for src, nxt, flat, turned in ((q_ref, qn, qb, qt), (g_ref, gn, gb, gt)):
                if g < groups - 1:
                    rows = src[b, pl.ds(BLOCK * g, 2 * BLOCK)]
                else:
                    rows = jnp.concatenate([src[b, pl.ds(BLOCK * g, BLOCK)], nxt[b]], axis=0)
                block = nn(take, rows).astype(bf16)
                flat[i] = block
                turned[i] = nt(eye, block).astype(bf16)

    def encode(slot, row):
        block = slot_block[slot]
        rows = recv[slot]
        scores = nt(s_ref[block], rows) * scale
        top = jnp.max(scores, axis=0, keepdims=True)
        raised = jnp.exp(scores - top)
        weights = raised / jnp.sum(raised, axis=0, keepdims=True)
        total = nn(st[block], weights.astype(bf16)) + nt(eye, rows)
        wts[slot] = weights
        summed[slot] = total
        squares[row[0], 0, pl.ds(row[1], 1), :] = jnp.sum(total * total, axis=0, keepdims=True)

    chunks = members // chunk
    rows_chunk = chunk * SLOTS

    def send_squares(c):
        def one(q, x):
            pltpu.make_async_remote_copy(
                src_ref=squares.at[c, 0], dst_ref=squares.at[c, q], send_sem=sq_send, recv_sem=sq_recv.at[c],
                device_id=plane(q), device_id_type=MESH,
            ).start()
            return x
        lax.fori_loop(1, peers, one, 0)

    for k in range(SLOTS):
        encode(k, (0, k))

    def encode_chunk(c, x):
        def one(p, y):
            pltpu.make_async_copy(
                recv.at[pl.ds(SLOTS * p, SLOTS)], recv.at[pl.ds(SLOTS * p, SLOTS)], data_recv.at[p]
            ).wait()
            for k in range(SLOTS):
                encode(SLOTS * p + k, (c, SLOTS * (p - c * chunk) + k))
            return y
        lax.fori_loop(jnp.maximum(c * chunk, 1), (c + 1) * chunk, one, 0)
        send_squares(c)
        return x

    lax.fori_loop(0, chunks, encode_chunk, 0)

    def finish_squares(c, x):
        pltpu.make_async_copy(
            squares.at[c, pl.ds(1, peers - 1)], squares.at[c, pl.ds(1, peers - 1)], sq_recv.at[c]
        ).wait()
        total = jnp.sum(squares[c], axis=0)
        inv[pl.ds(rows_chunk * c, rows_chunk), :] = lax.rsqrt(total / width + norm_eps)
        return x

    lax.fori_loop(0, chunks, finish_squares, 0)

    def attend(b, g):
        i = b * groups + g
        item = (g * seqs + b) * NBR
        normed = []
        for n in range(NBR):
            slot = item_slot[item + n]
            normed.append(summed[slot] * inv[pl.ds(slot, 1), :])
        normed = jnp.concatenate(normed, axis=1)
        keys = normed.astype(bf16)
        scores = nn(qb[i], keys) * scale
        raised = jnp.exp(scores - jnp.max(scores, axis=1, keepdims=True))
        weights = raised / jnp.sum(raised, axis=1, keepdims=True)
        low = weights.astype(bf16)
        atb[g + 1, b] = nt(low, keys).astype(bf16)
        wgrad = nn(gb[i], keys)
        slow = (weights * (wgrad - jnp.sum(weights * wgrad, axis=1, keepdims=True))).astype(bf16)
        qgb[g + 1, b] = (scale * nt(slow, keys)).astype(bf16)
        grad = (nn(gt[i], low) + scale * nn(qt[i], slow)).astype(bf16)
        kgrad[i] = grad
        inner = jnp.sum(grad.astype(f32) * normed, axis=0, keepdims=True)
        for n in range(NBR):
            proj[g, 0, pl.ds(NBR * b + n, 1), :] = inner[:, n * NLEN:(n + 1) * NLEN]

    def encode_grad(b, g):
        i = b * groups + g
        item = (g * seqs + b) * NBR
        total = None
        for n in range(NBR):
            slot = item_slot[item + n]
            scaled = inv[pl.ds(slot, 1), :]
            row = jnp.sum(proj[g, :, NBR * b + n, :], axis=0, keepdims=True) / width
            grad = kgrad[i, :, pl.ds(n * NLEN, NLEN)].astype(f32)
            sgrad = (scaled * (grad - summed[slot] * scaled * row)).astype(bf16)
            weights = wts[slot]
            wgrad = nn(s_ref[i], sgrad)
            slow = (weights * (wgrad - jnp.sum(weights * wgrad, axis=0, keepdims=True))).astype(bf16)
            term = nt(weights.astype(bf16), sgrad) + scale * nn(slow, recv[slot])
            term = term.astype(bf16).astype(f32)
            total = term if total is None else total + term
        sg_ref[b, pl.ds(g * BLOCK, BLOCK)] = total.astype(bf16)

    order = [groups - 1] + list(range(groups - 1))
    o_copies = []
    for g in order:
        for b in range(seqs):
            attend(b, g)
        if g == groups - 1:
            for k, buf in enumerate((atb, qgb)):
                copy = pltpu.make_async_remote_copy(
                    src_ref=buf.at[groups], dst_ref=buf.at[0], send_sem=o_send.at[k], recv_sem=o_recv.at[k],
                    device_id={"seq": after}, device_id_type=MESH,
                )
                copy.start()
                o_copies.append(copy)

        def send_proj(q, x, g=g):
            pltpu.make_async_remote_copy(
                src_ref=proj.at[g, 0], dst_ref=proj.at[g, q], send_sem=pr_send, recv_sem=pr_recv.at[g],
                device_id=plane(q), device_id_type=MESH,
            ).start()
            return x

        lax.fori_loop(1, peers, send_proj, 0)

    for g in order:
        pltpu.make_async_copy(
            proj.at[g, pl.ds(1, peers - 1)], proj.at[g, pl.ds(1, peers - 1)], pr_recv.at[g]
        ).wait()
        for b in range(seqs):
            encode_grad(b, g)

    for copy in o_copies:
        copy.wait()
    back = shift_matrix(BLOCK, 2 * BLOCK, 1)
    for buf, out in ((atb, att_ref), (qgb, qg_ref)):
        for b in range(seqs):
            buf[0, b] = (buf[0, b].astype(f32) * first).astype(bf16)
        for g in range(groups):
            for b in range(seqs):
                rows = jnp.concatenate([buf[g, b], buf[g + 1, b]], axis=0)
                out[b, pl.ds(g * BLOCK, BLOCK)] = nn(back, rows).astype(bf16)

    pltpu.make_async_copy(ids_in.at[pl.ds(1, members - 1)], ids_in.at[pl.ds(1, members - 1)], ids_send).wait()
    pltpu.make_async_copy(
        send.at[pl.ds(SLOTS, SLOTS * (members - 1))], send.at[pl.ds(SLOTS, SLOTS * (members - 1))], data_send
    ).wait()
    whole = squares.at[pl.ds(0, chunks), pl.ds(1, peers - 1)]
    pltpu.make_async_copy(whole, whole, sq_send).wait()
    whole = proj.at[pl.ds(0, groups), pl.ds(1, peers - 1)]
    pltpu.make_async_copy(whole, whole, pr_send).wait()


def on_device(members, ntp, ndp, queries, block_states, grad_out, store, owners, entries):
    seqs, rows, columns = queries.shape
    groups = rows // BLOCK
    blocks = seqs * groups
    items = blocks * NBR
    peers = ntp * ndp
    me = lax.axis_index("seq")
    flat_owner = owners.reshape(items)
    flat_entry = entries.reshape(items)

    distance = (me - flat_owner + members) % members
    half = members // 2
    step = distance - half
    place = jnp.where(step > 0, 2 * step + 1, jnp.where(step == 0, 1, -2 * step))
    place = jnp.where(distance == 0, 0, place)
    number = jnp.arange(items, dtype=jnp.int32)
    same = (flat_owner[:, None] == flat_owner[None, :]) & (number[None, :] < number[:, None])
    item_slot = place * SLOTS + jnp.sum(same.astype(jnp.int32), axis=1)
    cells = jnp.arange(members * SLOTS, dtype=jnp.int32)
    held = cells[:, None] == item_slot[None, :]
    slot_ids = jnp.sum(jnp.where(held, flat_entry[None, :], 0), axis=1)
    pair = number // NBR
    block_index = (pair % seqs) * groups + pair // seqs
    slot_block = jnp.sum(jnp.where(held, block_index[None, :], 0), axis=1)
    ids_row = jnp.pad(slot_ids, (0, 128 - members * SLOTS)).reshape(1, 128)

    chunk = max(1, members // 4)
    chunks = members // chunk
    vmem, smem = pltpu.VMEM, pltpu.SMEM
    dma = pltpu.SemaphoreType.DMA
    in_vmem = pl.BlockSpec(memory_space=vmem)
    in_smem = pl.BlockSpec(memory_space=smem)
    out = jax.ShapeDtypeStruct((seqs, rows, columns), bf16)
    attended, query_grad, state_grad = pl.pallas_call(
        functools.partial(kernel, members, ntp, ndp, seqs, groups, chunk),
        out_shape=(out, out, out),
        in_specs=[in_smem] * 3 + [in_vmem] * 5,
        out_specs=(in_vmem,) * 3,
        scratch_shapes=[
            vmem((members, 1, 128), jnp.int32),
            smem((members, 1, 128), jnp.int32),
            vmem((members * SLOTS, NLEN, HD), bf16),
            vmem((members * SLOTS, NLEN, HD), bf16),
            vmem((members * SLOTS, HD, NLEN), f32),
            vmem((members * SLOTS, BLOCK, NLEN), f32),
            vmem((chunks, peers, chunk * SLOTS, NLEN), f32),
            vmem((members * SLOTS, NLEN), f32),
            vmem((seqs, BLOCK, HD), bf16),
            vmem((seqs, BLOCK, HD), bf16),
            vmem((blocks, BLOCK, HD), bf16),
            vmem((blocks, BLOCK, HD), bf16),
            vmem((blocks, HD, BLOCK), bf16),
            vmem((blocks, HD, BLOCK), bf16),
            vmem((blocks, HD, BLOCK), bf16),
            vmem((groups + 1, seqs, BLOCK, HD), bf16),
            vmem((groups + 1, seqs, BLOCK, HD), bf16),
            vmem((blocks, HD, NBR * NLEN), bf16),
            vmem((groups, peers, seqs * NBR, NLEN), f32),
            dma, dma, dma, dma((2,)), dma((2,)),
            dma, dma((members,)), dma, dma((chunks,)), dma, dma((groups,)),
            dma((2,)), dma((2,)),
        ],
        compiler_params=pltpu.CompilerParams(
            collective_id=0, has_side_effects=True, vmem_limit_bytes=40 * 1024 * 1024
        ),
    )(
        item_slot, slot_block, slot_ids, ids_row, queries, grad_out,
        block_states.reshape(blocks, BLOCK, columns), store,
    )
    return attended, query_grad, state_grad


def solution(mesh):
    members, ntp, ndp = (mesh.shape[a] for a in ("seq", "tp", "dp"))
    rows = P(None, "seq", ("tp", "dp"))
    return jax.shard_map(
        functools.partial(on_device, members, ntp, ndp),
        mesh=mesh,
        in_specs=(rows, rows, rows, P("seq", None, ("tp", "dp")), P("seq", None, None), P("seq", None, None)),
        out_specs=(rows, rows, rows),
        check_vma=False,
    )
```

time: 589 us -> 149 us (0.25)
  blocking collectives: 342 us -> 0 us
  Pallas kernels: 0 us -> 140 us
  waiting for transfers between devices: 117 us -> 0 us
  starting transfers between devices: 44.3 us -> 0 us
  matrix products: 41.6 us -> 0 us
  local copies, waits for them, and re-layouts: 28.1 us -> 7.74 us
  other arithmetic: 13.6 us -> 0.3 us
    all_to_all x2 -> x0, blocking collectives: 225 us -> none  [the longest x1 119 us: on_device(): lax.all_to_all(encoded.reshape(ids_in.shape + (NLEN, columns)), 'seq', sp...]
    pallas_call x0 -> x1, Pallas kernels: none -> 140 us  [on_device(): pl.pallas_call(functools.partial(kernel, members, ntp, ndp, seqs, groups,...]
    psum x2 -> x0, blocking collectives: 117 us -> none  [the longest x1 60.4 us: encode_rows(): squares = lax.psum(jnp.sum(summed * summed, axis=(-2, -1)), ('tp', 'dp'))]
    all_to_all x3 -> x0, waiting for transfers between devices: 111 us -> none  [the longest x1 52.2 us: on_device(): lax.all_to_all(state_term.reshape(ids_in.shape + (BLOCK, columns)), 'seq'...]
    all_to_all x3 -> x0, starting transfers between devices: 40.3 us -> none  [the longest x1 18.3 us: on_device(): lax.all_to_all(state_term.reshape(ids_in.shape + (BLOCK, columns)), 'seq'...]
    dot_general x14 -> x0, matrix products: 38.4 us -> none  [the longest x1 5.96 us: encode_rows(): jnp.einsum('...hqk,...khd->...qhd', low_weights, states, preferred_elemen...]
    convert_element_type x5 -> x0, local copies, waits for them, and re-layouts: 8.65 us -> none  [the longest x1 4.19 us: on_device(): send_grads = jnp.einsum('zi,ilw->zlw', place_low, local_grad.reshape(item...]
    reshape x3 -> x2, local copies, waits for them, and re-layouts: 6.42 us -> 0.1 us  [the longest x1 0.09 us: on_device(): flat_owner = owners.reshape(items)]
  transfers between devices with their start and end apart: 5 -> 0, of which waited for: 5 -> 0; matrix products, arithmetic and copies ran while one was open for 3% -> 0% of each run, Pallas kernels for 0% -> 0%
where the time goes in v1:
time: 149 us
  Pallas kernels  140 us (94%)
  local copies, waits for them, and re-layouts  7.74 us (5%)
    pallas_call x1, Pallas kernels, on_device(): pl.pallas_call(functools.partial(kernel, members, ntp, ndp, seqs, groups,...  140 us
    unnamed x17, local copies, waits for them, and re-layouts  7.56 us

profile of v1, /device:TPU:1, one launch (start us, length us, event | category | flops | bytes accessed | tf_op | source)
XLA Modules:
  0.0 149.0 jit_solution(18062863351996529194)
XLA Ops:
  0.6 0.0 copy-start.4
  0.6 0.7 copy-done.4
  1.3 0.1 copy.13
  1.4 0.1 reshape.90
  1.5 0.0 copy-start.5
  1.5 0.2 convert_reduce_fusion
  1.7 0.5 copy-done.5
  2.2 0.1 copy.14
  2.3 0.1 broadcast_in_dim.30
  2.4 0.1 select_reduce_fusion
  2.5 0.0 copy-start
  2.5 1.2 copy-done
  3.8 0.0 copy-start.1
  3.8 0.9 copy-done.1
  4.7 0.0 copy-start.2
  4.7 0.9 copy-done.2
  5.7 0.0 copy-start.3
  5.7 0.9 copy-done.3
  6.6 140.3 %shard_map.85 = (bf16[4,256,128]{2,1,0:T(8,128)(2,1)S(1)}, bf16[4,256,128]{2,1,0:T(8,128)(2,1)S(1)}, bf16[4,256,128]{2,1,0:T(8,128)(2,1)S(1)}) custom-call(s32[32]{0:T(128)S(1)} %get-tuple-element.5.item_slot, s32[64]{0:T(128)S(1)} %get-tuple-element.4.slot_block, s32[64]{0:T(128)S(1)} %get-tuple-element.3.own_ids, s32[1,128]{1,0:T(1,128)S(1)} %pad_bitcast_fusion.ids_ref, ...), custom_call_target="tpu_custom_call" | custom-call | tf_op jit(solution)/shard_map/pallas_call | solution.py:318
  146.9 0.7 copy.18
  147.6 0.7 copy.19
  148.3 0.7 copy.20
  (2 shorter events, 0.0 us)
Async XLA Ops:
  0.6 0.7 copy-start.4
  1.5 0.7 copy-start.5
  2.5 1.2 copy-start
  3.8 0.9 copy-start.1
  4.7 0.9 copy-start.2
  5.7 0.9 copy-start.3

commit v2 on v1

--- a/solution.py
+++ b/solution.py
@@ -18,9 +18,17 @@
 bf16 = jnp.bfloat16
 
 
-def place_distance(place, members):
-    turn = members // 2 + (place // 2) * (1 - 2 * ((place + 1) % 2))
-    return turn
+def near_places(members):
+    return min(10, (members // 4) * 2)
+
+
+def near_distance(place, members):
+    return members + ((place + 1) // 2) * (1 - 2 * ((place + 1) % 2))
+
+
+def far_distance(place, members):
+    step = place - 1 - near_places(members)
+    return members // 2 + ((step + 1) // 2) * (1 - 2 * (step % 2))
 
 
 def nn(a, b):
@@ -39,10 +47,10 @@
 
 def kernel(
     members, ntp, ndp, seqs, groups, chunk,
-    item_slot, slot_block, own_ids, ids_ref, q_ref, g_ref, s_ref, store_ref,
+    item_slot, slot_block, own_ids, ids_ref, q_hbm, g_hbm, s_hbm, store_hbm,
     att_ref, qg_ref, sg_ref,
-    ids_in, ids_s, send, recv, summed, wts, squares, inv, qn, gn, qb, gb, qt, gt, st, atb, qgb, kgrad, proj,
-    ids_send, ids_recv, loc_sem, tok_send, tok_recv, data_send, data_recv, sq_send, sq_recv, pr_send, pr_recv,
+    q_ref, g_ref, s_ref, store_ref, ids_in, ids_s, send, recv, summed, ukeys, sraw, wraw, wts, squares, inv, qn, gn, qb, gb, qt, gt, st, kblk, atb, qgb, kgrad, proj,
+    in_sem, ids_send, ids_recv, loc_sem, tok_send, tok_recv, data_send, data_recv, sq_send, sq_recv, pr_send, pr_recv,
     o_send, o_recv,
 ):
     me = lax.axis_index("seq")
@@ -72,18 +80,26 @@
 
     lax.fori_loop(1, members, greet_ring, 0)
     lax.fori_loop(1, peers, greet_plane, 0)
+    loads = []
+    for k, (src, dst) in enumerate(((store_hbm, store_ref), (s_hbm, s_ref), (q_hbm, q_ref), (g_hbm, g_ref))):
+        load = pltpu.make_async_copy(src, dst, in_sem.at[k])
+        load.start()
+        loads.append(load)
     pl.semaphore_wait(barrier, members - 1 + peers - 1)
 
-    def send_ids(d, c):
-        pltpu.make_async_remote_copy(
-            src_ref=ids_ref, dst_ref=ids_in.at[d], send_sem=ids_send, recv_sem=ids_recv,
-            device_id=ring(d), device_id_type=MESH,
-        ).start()
-        return c
-
-    lax.fori_loop(1, members, send_ids, 0)
+    near = near_places(members)
+    parts = ((1, near + 1, near_distance), (near + 1, members, far_distance))
+    for k, (low, high, distance) in enumerate(parts):
+        def send_ids(p, c, k=k, distance=distance):
+            pltpu.make_async_remote_copy(
+                src_ref=ids_ref, dst_ref=ids_in.at[p], send_sem=ids_send, recv_sem=ids_recv.at[k],
+                device_id=ring(2 * members - distance(p, members)), device_id_type=MESH,
+            ).start()
+            return c
+
+        lax.fori_loop(low, high, send_ids, 0)
     tok_copies = []
-    for k, (src, dst) in enumerate(((q_ref, qn), (g_ref, gn))):
+    for k, (src, dst) in enumerate(((q_hbm, qn), (g_hbm, gn))):
         copy = pltpu.make_async_remote_copy(
             src_ref=src.at[:, pl.ds(0, BLOCK)], dst_ref=dst, send_sem=tok_send.at[k], recv_sem=tok_recv.at[k],
             device_id={"seq": before}, device_id_type=MESH,
@@ -93,6 +109,8 @@
 
     eye = shift_matrix(HD, HD, 0)
 
+    for load in loads:
+        load.wait()
     for k in range(SLOTS):
         recv[k] = store_ref[own_ids[k]]
 
@@ -102,22 +120,23 @@
 
     lax.fori_loop(0, seqs * groups, turn_states, 0)
 
-    pltpu.make_async_copy(ids_in.at[pl.ds(1, members - 1)], ids_in.at[pl.ds(1, members - 1)], ids_recv).wait()
-    to_scalar = pltpu.make_async_copy(ids_in.at[pl.ds(1, members - 1)], ids_s.at[pl.ds(1, members - 1)], loc_sem)
-    to_scalar.start()
-    to_scalar.wait()
-
-    def send_items(p, c):
-        d = place_distance(p, members)
-        for k in range(SLOTS):
-            send[SLOTS * p + k] = store_ref[ids_s[members - d, 0, SLOTS * p + k]]
-        pltpu.make_async_remote_copy(
-            src_ref=send.at[pl.ds(SLOTS * p, SLOTS)], dst_ref=recv.at[pl.ds(SLOTS * p, SLOTS)],
-            send_sem=data_send, recv_sem=data_recv.at[p], device_id=ring(d), device_id_type=MESH,
-        ).start()
-        return c
-
-    lax.fori_loop(1, members, send_items, 0)
+    for k, (low, high, distance) in enumerate(parts):
+        rows = ids_in.at[pl.ds(low, high - low)]
+        pltpu.make_async_copy(rows, rows, ids_recv.at[k]).wait()
+        to_scalar = pltpu.make_async_copy(rows, ids_s.at[pl.ds(low, high - low)], loc_sem.at[k])
+        to_scalar.start()
+        to_scalar.wait()
+
+        def send_items(p, c, distance=distance):
+            for k in range(SLOTS):
+                send[SLOTS * p + k] = store_ref[ids_s[p, 0, SLOTS * p + k]]
+            pltpu.make_async_remote_copy(
+                src_ref=send.at[pl.ds(SLOTS * p, SLOTS)], dst_ref=recv.at[pl.ds(SLOTS * p, SLOTS)],
+                send_sem=data_send, recv_sem=data_recv.at[p], device_id=ring(distance(p, members)), device_id_type=MESH,
+            ).start()
+            return c
+
+        lax.fori_loop(low, high, send_items, 0)
 
     for copy in tok_copies:
         copy.wait()
@@ -149,6 +168,7 @@
         total = nn(st[block], weights.astype(bf16)) + nt(eye, rows)
         wts[slot] = weights
         summed[slot] = total
+        ukeys[slot] = total.astype(bf16)
         squares[row[0], 0, pl.ds(row[1], 1), :] = jnp.sum(total * total, axis=0, keepdims=True)
 
     chunks = members // chunk
@@ -180,6 +200,19 @@
 
     lax.fori_loop(0, chunks, encode_chunk, 0)
 
+    def raw_scores(b, g):
+        i = b * groups + g
+        item = (g * seqs + b) * NBR
+        keys = jnp.concatenate([ukeys[item_slot[item + n]] for n in range(NBR)], axis=1)
+        kblk[i] = keys
+        sraw[i] = nn(qb[i], keys)
+        wraw[i] = nn(gb[i], keys)
+
+    order = [groups - 1] + list(range(groups - 1))
+    for g in order:
+        for b in range(seqs):
+            raw_scores(b, g)
+
     def finish_squares(c, x):
         pltpu.make_async_copy(
             squares.at[c, pl.ds(1, peers - 1)], squares.at[c, pl.ds(1, peers - 1)], sq_recv.at[c]
@@ -193,23 +226,20 @@
     def attend(b, g):
         i = b * groups + g
         item = (g * seqs + b) * NBR
-        normed = []
-        for n in range(NBR):
-            slot = item_slot[item + n]
-            normed.append(summed[slot] * inv[pl.ds(slot, 1), :])
-        normed = jnp.concatenate(normed, axis=1)
-        keys = normed.astype(bf16)
-        scores = nn(qb[i], keys) * scale
+        slots = [item_slot[item + n] for n in range(NBR)]
+        scaled = jnp.concatenate([inv[pl.ds(slot, 1), :] for slot in slots], axis=1)
+        keys = kblk[i]
+        scores = sraw[i] * (scaled * scale)
         raised = jnp.exp(scores - jnp.max(scores, axis=1, keepdims=True))
         weights = raised / jnp.sum(raised, axis=1, keepdims=True)
-        low = weights.astype(bf16)
-        atb[g + 1, b] = nt(low, keys).astype(bf16)
-        wgrad = nn(gb[i], keys)
-        slow = (weights * (wgrad - jnp.sum(weights * wgrad, axis=1, keepdims=True))).astype(bf16)
-        qgb[g + 1, b] = (scale * nt(slow, keys)).astype(bf16)
-        grad = (nn(gt[i], low) + scale * nn(qt[i], slow)).astype(bf16)
+        atb[g + 1, b] = nt((weights * scaled).astype(bf16), keys).astype(bf16)
+        wgrad = wraw[i] * scaled
+        sgrad = weights * (wgrad - jnp.sum(weights * wgrad, axis=1, keepdims=True))
+        qgb[g + 1, b] = (scale * nt((sgrad * scaled).astype(bf16), keys)).astype(bf16)
+        grad = (nn(gt[i], weights.astype(bf16)) + scale * nn(qt[i], sgrad.astype(bf16))).astype(bf16)
         kgrad[i] = grad
-        inner = jnp.sum(grad.astype(f32) * normed, axis=0, keepdims=True)
+        totals = jnp.concatenate([summed[slot] for slot in slots], axis=1)
+        inner = scaled * jnp.sum(grad.astype(f32) * totals, axis=0, keepdims=True)
         for n in range(NBR):
             proj[g, 0, pl.ds(NBR * b + n, 1), :] = inner[:, n * NLEN:(n + 1) * NLEN]
 
@@ -222,7 +252,7 @@
             scaled = inv[pl.ds(slot, 1), :]
             row = jnp.sum(proj[g, :, NBR * b + n, :], axis=0, keepdims=True) / width
             grad = kgrad[i, :, pl.ds(n * NLEN, NLEN)].astype(f32)
-            sgrad = (scaled * (grad - summed[slot] * scaled * row)).astype(bf16)
+            sgrad = (grad * scaled - summed[slot] * (scaled * scaled * row)).astype(bf16)
             weights = wts[slot]
             wgrad = nn(s_ref[i], sgrad)
             slow = (weights * (wgrad - jnp.sum(weights * wgrad, axis=0, keepdims=True))).astype(bf16)
@@ -231,7 +261,6 @@
             total = term if total is None else total + term
         sg_ref[b, pl.ds(g * BLOCK, BLOCK)] = total.astype(bf16)
 
-    order = [groups - 1] + list(range(groups - 1))
     o_copies = []
     for g in order:
         for b in range(seqs):
@@ -293,9 +322,11 @@
     flat_entry = entries.reshape(items)
 
     distance = (me - flat_owner + members) % members
-    half = members // 2
+    half, reach = members // 2, near_places(members) // 2
     step = distance - half
-    place = jnp.where(step > 0, 2 * step + 1, jnp.where(step == 0, 1, -2 * step))
+    place = near_places(members) + jnp.where(step > 0, 2 * step + 1, jnp.where(step == 0, 1, -2 * step))
+    place = jnp.where(distance <= reach, 2 * distance - 1, place)
+    place = jnp.where(distance >= members - reach, 2 * (members - distance), place)
     place = jnp.where(distance == 0, 0, place)
     number = jnp.arange(items, dtype=jnp.int32)
     same = (flat_owner[:, None] == flat_owner[None, :]) & (number[None, :] < number[:, None])
@@ -318,14 +349,21 @@
     attended, query_grad, state_grad = pl.pallas_call(
         functools.partial(kernel, members, ntp, ndp, seqs, groups, chunk),
         out_shape=(out, out, out),
-        in_specs=[in_smem] * 3 + [in_vmem] * 5,
+        in_specs=[in_smem] * 3 + [in_vmem] + [pl.BlockSpec(memory_space=pltpu.HBM)] * 4,
         out_specs=(in_vmem,) * 3,
         scratch_shapes=[
+            vmem(queries.shape, bf16),
+            vmem(queries.shape, bf16),
+            vmem((blocks, BLOCK, columns), bf16),
+            vmem(store.shape, bf16),
             vmem((members, 1, 128), jnp.int32),
             smem((members, 1, 128), jnp.int32),
             vmem((members * SLOTS, NLEN, HD), bf16),
             vmem((members * SLOTS, NLEN, HD), bf16),
             vmem((members * SLOTS, HD, NLEN), f32),
+            vmem((members * SLOTS, HD, NLEN), bf16),
+            vmem((blocks, BLOCK, NBR * NLEN), f32),
+            vmem((blocks, BLOCK, NBR * NLEN), f32),
             vmem((members * SLOTS, BLOCK, NLEN), f32),
             vmem((chunks, peers, chunk * SLOTS, NLEN), f32),
             vmem((members * SLOTS, NLEN), f32),
@@ -336,16 +374,17 @@
             vmem((blocks, HD, BLOCK), bf16),
             vmem((blocks, HD, BLOCK), bf16),
             vmem((blocks, HD, BLOCK), bf16),
+            vmem((blocks, HD, NBR * NLEN), bf16),
             vmem((groups + 1, seqs, BLOCK, HD), bf16),
             vmem((groups + 1, seqs, BLOCK, HD), bf16),
             vmem((blocks, HD, NBR * NLEN), bf16),
             vmem((groups, peers, seqs * NBR, NLEN), f32),
-            dma, dma, dma, dma((2,)), dma((2,)),
+            dma((4,)), dma, dma((2,)), dma((2,)), dma((2,)), dma((2,)),
             dma, dma((members,)), dma, dma((chunks,)), dma, dma((groups,)),
             dma((2,)), dma((2,)),
         ],
         compiler_params=pltpu.CompilerParams(
-            collective_id=0, has_side_effects=True, vmem_limit_bytes=40 * 1024 * 1024
+            collective_id=0, has_side_effects=True, vmem_limit_bytes=48 * 1024 * 1024
         ),
     )(
         item_slot, slot_block, slot_ids, ids_row, queries, grad_out,

time: 149 us -> 141 us (0.946)
  Pallas kernels: 140 us -> 131 us
    pallas_call x1, Pallas kernels: 140 us -> 131 us  [on_device(): pl.pallas_call(functools.partial(kernel, members, ntp, ndp, seqs, groups,...]
where the time goes in v2:
time: 141 us; the launch traced here: 140 us
  Pallas kernels  131 us (93%)
  local copies, waits for them, and re-layouts  7.74 us (5%)
    pallas_call x1, Pallas kernels, on_device(): pl.pallas_call(functools.partial(kernel, members, ntp, ndp, seqs, groups,...  131 us
    unnamed x17, local copies, waits for them, and re-layouts  7.55 us

profile of v2, /device:TPU:1, one launch (start us, length us, event | category | flops | bytes accessed | tf_op | source)
XLA Modules:
  0.0 139.6 jit_solution(5441286983324315724)
XLA Ops:
  0.6 0.0 copy-start.4
  0.6 0.7 copy-done.4
  1.3 0.1 copy.13
  1.4 0.1 reshape.99
  1.5 0.0 copy-start.5
  1.5 0.2 convert_reduce_fusion
  1.7 0.5 copy-done.5
  2.2 0.1 copy.14
  2.3 0.1 broadcast_in_dim.30
  2.4 0.1 select_reduce_fusion
  2.5 0.0 copy-start
  2.5 1.2 copy-done
  3.8 0.0 copy-start.1
  3.8 0.9 copy-done.1
  4.7 0.0 copy-start.2
  4.7 0.9 copy-done.2
  5.7 0.0 copy-start.3
  5.7 0.9 copy-done.3
  6.6 130.9 %shard_map.85 = (bf16[4,256,128]{2,1,0:T(8,128)(2,1)S(1)}, bf16[4,256,128]{2,1,0:T(8,128)(2,1)S(1)}, bf16[4,256,128]{2,1,0:T(8,128)(2,1)S(1)}) custom-call(s32[32]{0:T(128)S(1)} %get-tuple-element.5.item_slot, s32[64]{0:T(128)S(1)} %get-tuple-element.4.slot_block, s32[64]{0:T(128)S(1)} %get-tuple-element.3.own_ids, s32[1,128]{1,0:T(1,128)S(1)} %pad_bitcast_fusion.ids_ref, ...), custom_call_target="tpu_custom_call" | custom-call | tf_op jit(solution)/shard_map/pallas_call | solution.py:349
  137.5 0.7 copy.18
  138.2 0.7 copy.19
  138.9 0.7 copy.20
  (2 shorter events, 0.0 us)
Async XLA Ops:
  0.6 0.7 copy-start.4
  1.5 0.7 copy-start.5
  2.5 1.2 copy-start
  3.8 0.9 copy-start.1
  4.7 0.9 copy-start.2
  5.7 0.9 copy-start.3

commit v3 on v2

--- a/solution.py
+++ b/solution.py
@@ -31,6 +31,15 @@
     return members // 2 + ((step + 1) // 2) * (1 - 2 * (step % 2))
 
 
+def owner_place(distance, members):
+    reach = near_places(members) // 2
+    step = distance - members // 2
+    place = near_places(members) + jnp.where(step > 0, 2 * step + 1, jnp.where(step == 0, 1, -2 * step))
+    place = jnp.where(distance <= reach, 2 * distance - 1, place)
+    place = jnp.where(distance >= members - reach, 2 * (members - distance), place)
+    return jnp.where(distance == 0, 0, place)
+
+
 def nn(a, b):
     return lax.dot_general(a, b, (((1,), (0,)), ((), ())), preferred_element_type=f32)
 
@@ -46,11 +55,12 @@
 
 
 def kernel(
-    members, ntp, ndp, seqs, groups, chunk,
-    item_slot, slot_block, own_ids, ids_ref, q_hbm, g_hbm, s_hbm, store_hbm,
+    members, ntp, ndp, seqs, groups, chunks,
+    owners_hbm, entries_hbm, q_hbm, g_hbm, s_hbm, store_hbm,
     att_ref, qg_ref, sg_ref,
+    owner_s, entry_s, slots, plan, ids_ref, slot_s, plan_s,
     q_ref, g_ref, s_ref, store_ref, ids_in, ids_s, send, recv, summed, ukeys, sraw, wraw, wts, squares, inv, qn, gn, qb, gb, qt, gt, st, kblk, atb, qgb, kgrad, proj,
-    in_sem, ids_send, ids_recv, loc_sem, tok_send, tok_recv, data_send, data_recv, sq_send, sq_recv, pr_send, pr_recv,
+    plan_sem, in_sem, ids_send, ids_recv, loc_sem, tok_send, tok_recv, data_send, data_recv, sq_send, sq_recv, pr_send, pr_recv,
     o_send, o_recv,
 ):
     me = lax.axis_index("seq")
@@ -80,11 +90,46 @@
 
     lax.fori_loop(1, members, greet_ring, 0)
     lax.fori_loop(1, peers, greet_plane, 0)
+    tables = []
+    for k, (src, dst) in enumerate(((owners_hbm, owner_s), (entries_hbm, entry_s))):
+        table = pltpu.make_async_copy(src, dst, plan_sem.at[k])
+        table.start()
+        tables.append(table)
     loads = []
     for k, (src, dst) in enumerate(((store_hbm, store_ref), (s_hbm, s_ref), (q_hbm, q_ref), (g_hbm, g_ref))):
         load = pltpu.make_async_copy(src, dst, in_sem.at[k])
         load.start()
         loads.append(load)
+
+    for table in tables:
+        table.wait()
+    items = groups * NBR * seqs
+    row = lax.broadcasted_iota(jnp.int32, (items, 128), 0)
+    lane = lax.broadcasted_iota(jnp.int32, (items, 128), 1)
+    owner = jnp.zeros((items, 128), jnp.int32)
+    entry = jnp.zeros((items, 128), jnp.int32)
+    rank = jnp.zeros((items, 128), jnp.int32)
+    flat = [(g, n, b) for g in range(groups) for n in range(NBR) for b in range(seqs)]
+    for i, at in enumerate(flat):
+        owner = jnp.where(row == i, owner_s[at], owner)
+        entry = jnp.where(row == i, entry_s[at], entry)
+    for i, at in enumerate(flat):
+        rank = jnp.where((row > i) & (owner == owner_s[at]), rank + 1, rank)
+    slot = owner_place(lax.rem(me - owner + members, members), members) * SLOTS + rank
+    slot = jnp.clip(slot, 0, members * SLOTS - 1)
+    group = row // (NBR * seqs)
+    held = slot == lane
+    slots[...] = slot
+    wanted = jnp.sum(jnp.where(held, entry, 0), axis=0, keepdims=True)
+    ids_ref[...] = jnp.clip(wanted, 0, store_ref.shape[0] - 1)
+    plan[0:1, :] = ids_ref[...]
+    whose = jnp.sum(jnp.where(held, (row % seqs) * groups + group, 0), axis=0, keepdims=True)
+    plan[1:2, :] = jnp.clip(whose, 0, seqs * groups - 1)
+    scalars = []
+    for k, (src, dst) in enumerate(((plan, plan_s), (slots, slot_s))):
+        scalar = pltpu.make_async_copy(src, dst, plan_sem.at[2 + k])
+        scalar.start()
+        scalars.append(scalar)
     pl.semaphore_wait(barrier, members - 1 + peers - 1)
 
     near = near_places(members)
@@ -109,10 +154,10 @@
 
     eye = shift_matrix(HD, HD, 0)
 
-    for load in loads:
+    for load in loads + scalars:
         load.wait()
     for k in range(SLOTS):
-        recv[k] = store_ref[own_ids[k]]
+        recv[k] = store_ref[plan_s[0, k]]
 
     def turn_states(i, c):
         st[i] = nt(eye, s_ref[i]).astype(bf16)
@@ -158,8 +203,8 @@
                 flat[i] = block
                 turned[i] = nt(eye, block).astype(bf16)
 
-    def encode(slot, row):
-        block = slot_block[slot]
+    def encode(slot):
+        block = plan_s[1, slot]
         rows = recv[slot]
         scores = nt(s_ref[block], rows) * scale
         top = jnp.max(scores, axis=0, keepdims=True)
@@ -169,41 +214,38 @@
         wts[slot] = weights
         summed[slot] = total
         ukeys[slot] = total.astype(bf16)
-        squares[row[0], 0, pl.ds(row[1], 1), :] = jnp.sum(total * total, axis=0, keepdims=True)
-
-    chunks = members // chunk
-    rows_chunk = chunk * SLOTS
-
-    def send_squares(c):
+        squares[0, pl.ds(slot, 1), :] = jnp.sum(total * total, axis=0, keepdims=True)
+
+    def send_squares(c, low, high):
+        rows = pl.ds(SLOTS * low, SLOTS * (high - low))
+
         def one(q, x):
             pltpu.make_async_remote_copy(
-                src_ref=squares.at[c, 0], dst_ref=squares.at[c, q], send_sem=sq_send, recv_sem=sq_recv.at[c],
+                src_ref=squares.at[0, rows], dst_ref=squares.at[q, rows], send_sem=sq_send, recv_sem=sq_recv.at[c],
                 device_id=plane(q), device_id_type=MESH,
             ).start()
             return x
+
         lax.fori_loop(1, peers, one, 0)
 
     for k in range(SLOTS):
-        encode(k, (0, k))
-
-    def encode_chunk(c, x):
-        def one(p, y):
-            pltpu.make_async_copy(
-                recv.at[pl.ds(SLOTS * p, SLOTS)], recv.at[pl.ds(SLOTS * p, SLOTS)], data_recv.at[p]
-            ).wait()
-            for k in range(SLOTS):
-                encode(SLOTS * p + k, (c, SLOTS * (p - c * chunk) + k))
-            return y
-        lax.fori_loop(jnp.maximum(c * chunk, 1), (c + 1) * chunk, one, 0)
-        send_squares(c)
+        encode(k)
+
+    def take_place(p, x):
+        rows = recv.at[pl.ds(SLOTS * p, SLOTS)]
+        pltpu.make_async_copy(rows, rows, data_recv.at[p]).wait()
+        for k in range(SLOTS):
+            encode(SLOTS * p + k)
         return x
 
-    lax.fori_loop(0, chunks, encode_chunk, 0)
+    for c, (low, high) in enumerate(chunks):
+        lax.fori_loop(max(low, 1), high, take_place, 0)
+        send_squares(c, low, high)
 
     def raw_scores(b, g):
         i = b * groups + g
-        item = (g * seqs + b) * NBR
-        keys = jnp.concatenate([ukeys[item_slot[item + n]] for n in range(NBR)], axis=1)
+        item = g * NBR * seqs + b
+        keys = jnp.concatenate([ukeys[slot_s[item + n * seqs, 0]] for n in range(NBR)], axis=1)
         kblk[i] = keys
         sraw[i] = nn(qb[i], keys)
         wraw[i] = nn(gb[i], keys)
@@ -213,20 +255,16 @@
         for b in range(seqs):
             raw_scores(b, g)
 
-    def finish_squares(c, x):
-        pltpu.make_async_copy(
-            squares.at[c, pl.ds(1, peers - 1)], squares.at[c, pl.ds(1, peers - 1)], sq_recv.at[c]
-        ).wait()
-        total = jnp.sum(squares[c], axis=0)
-        inv[pl.ds(rows_chunk * c, rows_chunk), :] = lax.rsqrt(total / width + norm_eps)
-        return x
-
-    lax.fori_loop(0, chunks, finish_squares, 0)
+    for c, (low, high) in enumerate(chunks):
+        rows = pl.ds(SLOTS * low, SLOTS * (high - low))
+        sums = squares.at[pl.ds(1, peers - 1), rows]
+        pltpu.make_async_copy(sums, sums, sq_recv.at[c]).wait()
+        inv[rows, :] = lax.rsqrt(jnp.sum(squares[:, rows, :], axis=0) / width + norm_eps)
 
     def attend(b, g):
         i = b * groups + g
-        item = (g * seqs + b) * NBR
-        slots = [item_slot[item + n] for n in range(NBR)]
+        item = g * NBR * seqs + b
+        slots = [slot_s[item + n * seqs, 0] for n in range(NBR)]
         scaled = jnp.concatenate([inv[pl.ds(slot, 1), :] for slot in slots], axis=1)
         keys = kblk[i]
         scores = sraw[i] * (scaled * scale)
@@ -245,10 +283,10 @@
 
     def encode_grad(b, g):
         i = b * groups + g
-        item = (g * seqs + b) * NBR
+        item = g * NBR * seqs + b
         total = None
         for n in range(NBR):
-            slot = item_slot[item + n]
+            slot = slot_s[item + n * seqs, 0]
             scaled = inv[pl.ds(slot, 1), :]
             row = jnp.sum(proj[g, :, NBR * b + n, :], axis=0, keepdims=True) / width
             grad = kgrad[i, :, pl.ds(n * NLEN, NLEN)].astype(f32)
@@ -283,6 +321,17 @@
 
         lax.fori_loop(1, peers, send_proj, 0)
 
+    back = shift_matrix(BLOCK, 2 * BLOCK, 1)
+
+    def token_order(g):
+        for buf, out in ((atb, att_ref), (qgb, qg_ref)):
+            for b in range(seqs):
+                rows = jnp.concatenate([buf[g, b], buf[g + 1, b]], axis=0)
+                out[b, pl.ds(g * BLOCK, BLOCK)] = nn(back, rows).astype(bf16)
+
+    for g in range(1, groups):
+        token_order(g)
+
     for g in order:
         pltpu.make_async_copy(
             proj.at[g, pl.ds(1, peers - 1)], proj.at[g, pl.ds(1, peers - 1)], pr_recv.at[g]
@@ -292,20 +341,16 @@
 
     for copy in o_copies:
         copy.wait()
-    back = shift_matrix(BLOCK, 2 * BLOCK, 1)
-    for buf, out in ((atb, att_ref), (qgb, qg_ref)):
+    for buf in (atb, qgb):
         for b in range(seqs):
             buf[0, b] = (buf[0, b].astype(f32) * first).astype(bf16)
-        for g in range(groups):
-            for b in range(seqs):
-                rows = jnp.concatenate([buf[g, b], buf[g + 1, b]], axis=0)
-                out[b, pl.ds(g * BLOCK, BLOCK)] = nn(back, rows).astype(bf16)
+    token_order(0)
 
     pltpu.make_async_copy(ids_in.at[pl.ds(1, members - 1)], ids_in.at[pl.ds(1, members - 1)], ids_send).wait()
     pltpu.make_async_copy(
         send.at[pl.ds(SLOTS, SLOTS * (members - 1))], send.at[pl.ds(SLOTS, SLOTS * (members - 1))], data_send
     ).wait()
-    whole = squares.at[pl.ds(0, chunks), pl.ds(1, peers - 1)]
+    whole = squares.at[pl.ds(1, peers - 1)]
     pltpu.make_async_copy(whole, whole, sq_send).wait()
     whole = proj.at[pl.ds(0, groups), pl.ds(1, peers - 1)]
     pltpu.make_async_copy(whole, whole, pr_send).wait()
@@ -317,41 +362,24 @@
     blocks = seqs * groups
     items = blocks * NBR
     peers = ntp * ndp
-    me = lax.axis_index("seq")
-    flat_owner = owners.reshape(items)
-    flat_entry = entries.reshape(items)
-
-    distance = (me - flat_owner + members) % members
-    half, reach = members // 2, near_places(members) // 2
-    step = distance - half
-    place = near_places(members) + jnp.where(step > 0, 2 * step + 1, jnp.where(step == 0, 1, -2 * step))
-    place = jnp.where(distance <= reach, 2 * distance - 1, place)
-    place = jnp.where(distance >= members - reach, 2 * (members - distance), place)
-    place = jnp.where(distance == 0, 0, place)
-    number = jnp.arange(items, dtype=jnp.int32)
-    same = (flat_owner[:, None] == flat_owner[None, :]) & (number[None, :] < number[:, None])
-    item_slot = place * SLOTS + jnp.sum(same.astype(jnp.int32), axis=1)
-    cells = jnp.arange(members * SLOTS, dtype=jnp.int32)
-    held = cells[:, None] == item_slot[None, :]
-    slot_ids = jnp.sum(jnp.where(held, flat_entry[None, :], 0), axis=1)
-    pair = number // NBR
-    block_index = (pair % seqs) * groups + pair // seqs
-    slot_block = jnp.sum(jnp.where(held, block_index[None, :], 0), axis=1)
-    ids_row = jnp.pad(slot_ids, (0, 128 - members * SLOTS)).reshape(1, 128)
-
-    chunk = max(1, members // 4)
-    chunks = members // chunk
+    bounds = sorted({0, members // 4, members // 2, members * 3 // 4, members * 7 // 8, members * 15 // 16, members})
+    chunks = list(zip(bounds[:-1], bounds[1:]))
     vmem, smem = pltpu.VMEM, pltpu.SMEM
     dma = pltpu.SemaphoreType.DMA
-    in_vmem = pl.BlockSpec(memory_space=vmem)
-    in_smem = pl.BlockSpec(memory_space=smem)
     out = jax.ShapeDtypeStruct((seqs, rows, columns), bf16)
     attended, query_grad, state_grad = pl.pallas_call(
-        functools.partial(kernel, members, ntp, ndp, seqs, groups, chunk),
+        functools.partial(kernel, members, ntp, ndp, seqs, groups, chunks),
         out_shape=(out, out, out),
-        in_specs=[in_smem] * 3 + [in_vmem] + [pl.BlockSpec(memory_space=pltpu.HBM)] * 4,
-        out_specs=(in_vmem,) * 3,
+        in_specs=[pl.BlockSpec(memory_space=pltpu.HBM)] * 6,
+        out_specs=(pl.BlockSpec(memory_space=vmem),) * 3,
         scratch_shapes=[
+            smem((groups, NBR, seqs), jnp.int32),
+            smem((groups, NBR, seqs), jnp.int32),
+            vmem((items, 128), jnp.int32),
+            vmem((8, 128), jnp.int32),
+            vmem((1, 128), jnp.int32),
+            smem((items, 128), jnp.int32),
+            smem((8, 128), jnp.int32),
             vmem(queries.shape, bf16),
             vmem(queries.shape, bf16),
             vmem((blocks, BLOCK, columns), bf16),
@@ -365,7 +393,7 @@
             vmem((blocks, BLOCK, NBR * NLEN), f32),
             vmem((blocks, BLOCK, NBR * NLEN), f32),
             vmem((members * SLOTS, BLOCK, NLEN), f32),
-            vmem((chunks, peers, chunk * SLOTS, NLEN), f32),
+            vmem((peers, members * SLOTS, NLEN), f32),
             vmem((members * SLOTS, NLEN), f32),
             vmem((seqs, BLOCK, HD), bf16),
             vmem((seqs, BLOCK, HD), bf16),
@@ -379,18 +407,30 @@
             vmem((groups + 1, seqs, BLOCK, HD), bf16),
             vmem((blocks, HD, NBR * NLEN), bf16),
             vmem((groups, peers, seqs * NBR, NLEN), f32),
-            dma((4,)), dma, dma((2,)), dma((2,)), dma((2,)), dma((2,)),
-            dma, dma((members,)), dma, dma((chunks,)), dma, dma((groups,)),
+            dma((4,)), dma((4,)), dma, dma((2,)), dma((2,)), dma((2,)), dma((2,)),
+            dma, dma((members,)), dma, dma((len(chunks),)), dma, dma((groups,)),
             dma((2,)), dma((2,)),
         ],
         compiler_params=pltpu.CompilerParams(
-            collective_id=0, has_side_effects=True, vmem_limit_bytes=48 * 1024 * 1024
+            collective_id=0, has_side_effects=True, vmem_limit_bytes=62690000
         ),
     )(
-        item_slot, slot_block, slot_ids, ids_row, queries, grad_out,
+        jnp.transpose(owners, (0, 2, 1)), jnp.transpose(entries, (0, 2, 1)), queries, grad_out,
         block_states.reshape(blocks, BLOCK, columns), store,
     )
-    return attended, query_grad, state_grad
+    def hand_on(a_in, q_in, s_in, a_out, q_out, s_out, sems):
+        copies = []
+        for k, (src, dst) in enumerate(((a_in, a_out), (q_in, q_out), (s_in, s_out))):
+            copy = pltpu.make_async_copy(src, dst, sems.at[k])
+            copy.start()
+            copies.append(copy)
+        for copy in copies:
+            copy.wait()
+
+    hbm = pl.BlockSpec(memory_space=pltpu.HBM)
+    return pl.pallas_call(
+        hand_on, out_shape=(out, out, out), in_specs=[pl.BlockSpec(memory_space=vmem)] * 3, out_specs=(hbm,) * 3, scratch_shapes=[dma((3,))],
+    )(attended, query_grad, state_grad)
 
 
 def solution(mesh):

time: 141 us -> 135 us (0.957)
  local copies, waits for them, and re-layouts: 7.74 us -> 0 us
  Pallas kernels: 131 us -> 133 us
    unnamed x17 -> x0, local copies, waits for them, and re-layouts: 7.55 us -> none
    pallas_call x0 -> x1, Pallas kernels: none -> 2.01 us  [on_device(): pl.pallas_call(hand_on, out_shape=(out, out, out), in_specs=[pl.BlockSpec...]
where the time goes in v3:
time: 135 us; the launch traced here: 133 us
  Pallas kernels  133 us (99%)
    pallas_call x1, Pallas kernels, on_device(): pl.pallas_call(functools.partial(kernel, members, ntp, ndp, seqs, groups,...  131 us

profile of v3, /device:TPU:1, one launch (start us, length us, event | category | flops | bytes accessed | tf_op | source)
XLA Modules:
  0.0 133.5 jit_solution(17485673156691227020)
XLA Ops:
  0.6 130.8 %shard_map.85 = (bf16[4,256,128]{2,1,0:T(8,128)(2,1)}, bf16[4,256,128]{2,1,0:T(8,128)(2,1)}, bf16[4,256,128]{2,1,0:T(8,128)(2,1)}) custom-call(s32[4,2,4]{2,1,0:T(2,128)} %bitcast.4, s32[4,2,4]{2,1,0:T(2,128)} %bitcast.5, bf16[4,256,128]{2,1,0:T(8,128)(2,1)} %q_hbm.1, bf16[4,256,128]{2,1,0:T(8,128)(2,1)} %g_hbm.1, bf16[16,64,128]{2,1,0:T(8,128)(2,1)} %bitcast.3, ...), custom_call_target="tpu_custom_call" | custom-call | tf_op jit(solution)/shard_map/pallas_call | solution.py:370
  131.5 2.0 %shard_map.86 = (bf16[4,256,128]{2,1,0:T(8,128)(2,1)}, bf16[4,256,128]{2,1,0:T(8,128)(2,1)}, bf16[4,256,128]{2,1,0:T(8,128)(2,1)}) custom-call(bf16[4,256,128]{2,1,0:T(8,128)(2,1)} %get-tuple-element.6.a_in, bf16[4,256,128]{2,1,0:T(8,128)(2,1)} %get-tuple-element.7.q_in, bf16[4,256,128]{2,1,0:T(8,128)(2,1)} %get-tuple-element.8.s_in), custom_call_target="tpu_custom_call" | custom-call | tf_op jit(solution)/shard_map/pallas_call | solution.py:431
